TPU v7x, 32 devices: a whole 2x2x4 slice. The times are simulated.
32 devices in a mesh: shard: 32 (over z, y, x, core).
Axes of the slice: x: 2, y: 2, z: 4, core: 2. Of those that a mesh axis runs over, the one named last changes fastest.
Arguments:
- features: bfloat16 [163840, 400], P('shard'), may hold values from -6 to 6
- counts: int32 [32], P('shard'), may hold values from 1706 to 5120, as said below
- labelled: int32 [163840], P('shard'), may hold values from 0 to 1, as said below
- labels: int32 [163840], P('shard'), may hold values from 0 to 46
- w_branch: float32 [400, 512], P(None, 'shard'), may hold values from -0.625 to 0.625
- w_mid: float32 [2048, 512], P(None, 'shard'), may hold values from -0.125 to 0.125
- w_head: float32 [512, 47], replicated, may hold values from -0.25 to 0.25
- small_params: float32 [9775], replicated, as said below
- mom_branch: float32 [400, 512], P(None, 'shard'), may hold values from -16 to 16
- mom_mid: float32 [2048, 512], P(None, 'shard'), may hold values from -28 to 28
- mom_head: float32 [512, 47], replicated, may hold values from -3072 to 3072
- mom_small: float32 [9775], replicated, may hold values from -20 to 20
- avg_branch: float32 [400, 512], P(None, 'shard'), may hold values from -0.625 to 0.625
- avg_mid: float32 [2048, 512], P(None, 'shard'), may hold values from -0.125 to 0.125
- avg_head: float32 [512, 47], replicated, may hold values from -0.25 to 0.25
- avg_small: float32 [9775], replicated, may hold values from -3 to 3
Outputs:
- logits: float32 [163840, 47], P('shard')
- features_grad: float32 [163840, 400], P('shard')
- grad_branch: float32 [400, 512], P(None, 'shard')
- grad_mid: float32 [2048, 512], P(None, 'shard')
- grad_head: float32 [512, 47], replicated
- grad_small: float32 [9775], replicated
- new_mom_branch: float32 [400, 512], P(None, 'shard')
- new_mom_mid: float32 [2048, 512], P(None, 'shard')
- new_mom_head: float32 [512, 47], replicated
- new_mom_small: float32 [9775], replicated
- new_avg_branch: float32 [400, 512], P(None, 'shard')
- new_avg_mid: float32 [2048, 512], P(None, 'shard')
- new_avg_head: float32 [512, 47], replicated
- new_avg_small: float32 [9775], replicated
- new_branch: float32 [400, 512], P(None, 'shard')
- new_mid: float32 [2048, 512], P(None, 'shard')
- new_head: float32 [512, 47], replicated
- new_small: float32 [9775], replicated
Inputs may be any that keep to these rules, and one draw needn't show every extreme that they name: `counts`: filled slots of each device's bucket; some device's bucket is full in every draw. `labelled`: the first slot of every device's bucket is a training node. `small_params`: gains near one, shifts and class bias of both signs, slopes between 0.05 and 0.45.
All inputs are finite; a program needn't handle non-finite values.
Results may differ from a plain program's by a relative error of at most 0.0076.
Values may be sent and summed in bfloat16 or wider, within the bound.
A program may use at most 320 MiB of HBM per device.

v0:
```python
import math
import jax
import jax.numpy as jnp
from jax import lax
from jax.sharding import PartitionSpec as P

K = 4
F = 100
H = 512
C = 47
EPS = 1e-05
MOMENTUM = 0.9
DECAY = 0.9


def prelu_apply(values_in, slopes):
    return slopes * values_in + (1.0 - slopes) * jax.nn.softplus(values_in)


def prelu_slope_term(values_in):
    return values_in - jax.nn.softplus(values_in)


def prelu_input_factor(values_in, slopes):
    return slopes + (1.0 - slopes) * jax.nn.sigmoid(values_in)


def split_small(packed):
    width = K * H
    return (
        packed[:width],
        packed[width : 2 * width],
        packed[2 * width : 3 * width],
        packed[3 * width : 4 * width],
        packed[4 * width : 4 * width + H],
        packed[4 * width + H : 4 * width + 2 * H],
        packed[4 * width + 2 * H : 4 * width + 3 * H],
        packed[4 * width + 3 * H :],
    )


def nesterov(weight, gradient, momentum_old, average_old, step_rate):
    momentum_new = MOMENTUM * momentum_old + gradient
    weight_new = weight - step_rate * (gradient + MOMENTUM * momentum_new)
    average_new = DECAY * average_old + (1.0 - DECAY) * weight_new
    return (momentum_new, average_new, weight_new)


def moments(columns_in, bucket):
    masked = columns_in * bucket[:, None]
    totals, count_fill = lax.psum((jnp.sum(masked, axis=0), jnp.sum(bucket)), "shard")
    mean_col = totals / count_fill
    centered = columns_in - mean_col
    squares = lax.psum(jnp.sum(centered * centered * bucket[:, None], axis=0), "shard")
    variance = squares / count_fill
    return (mean_col, lax.rsqrt(variance + EPS), count_fill)


def local(
    features,
    counts,
    labelled,
    labels,
    w_branch,
    w_mid,
    w_head,
    small_params,
    mom_branch,
    mom_mid,
    mom_head,
    mom_small,
    avg_branch,
    avg_mid,
    avg_head,
    avg_small,
):
    node_rows = features.shape[0]
    nodes_all = node_rows * lax.axis_size("shard")
    gain1, shift1, slope1, slope2, gain2, shift2, slope3, head_bias = split_small(small_params)
    slot_index = lax.broadcasted_iota(jnp.int32, (node_rows,), 0)
    bucket = (slot_index < counts[0]).astype(jnp.float32)
    trained = bucket * labelled.astype(jnp.float32)
    branch_low = w_branch.astype(jnp.bfloat16)
    mid_low = w_mid.astype(jnp.bfloat16)
    head_low = w_head.astype(jnp.bfloat16)
    branch_full = lax.all_gather(branch_low, "shard", axis=1, tiled=True)
    feats_three = features.reshape(node_rows, K, F)
    branch_three = branch_full.reshape(K, F, H)
    branch_pre = jnp.einsum(
        "nkf,kfh->nkh", feats_three, branch_three, preferred_element_type=jnp.float32
    ).reshape(node_rows, K * H)
    mean1, inv1, count_fill = moments(branch_pre, bucket)
    branch_hat = (branch_pre - mean1) * inv1
    branch_norm = gain1 * branch_hat + shift1
    branch_act = prelu_apply(branch_norm, slope1)
    concat_low = prelu_apply(branch_act, slope2).astype(jnp.bfloat16)
    mid_full = lax.all_gather(mid_low, "shard", axis=1, tiled=True)
    mid_pre = jnp.dot(concat_low, mid_full, preferred_element_type=jnp.float32)
    mean2, inv2, unused_fill = moments(mid_pre, bucket)
    mid_hat = (mid_pre - mean2) * inv2
    mid_norm = gain2 * mid_hat + shift2
    hidden_low = prelu_apply(mid_norm, slope3).astype(jnp.bfloat16)
    scores = jnp.dot(hidden_low, head_low, preferred_element_type=jnp.float32) + head_bias
    log_total = jax.nn.logsumexp(scores, axis=1)
    prob_rows = jnp.exp(scores - log_total[:, None])
    one_hot = (labels[:, None] == lax.broadcasted_iota(jnp.int32, (1, C), 1)).astype(jnp.float32)
    logit_low = ((prob_rows - one_hot) * trained[:, None]).astype(jnp.bfloat16)
    head_part = jnp.dot(hidden_low.T, logit_low, preferred_element_type=jnp.float32)
    bias_part = jnp.sum(logit_low.astype(jnp.float32), axis=0)
    hidden_grad = jnp.dot(logit_low, head_low.T, preferred_element_type=jnp.float32)
    slope_out_part = jnp.sum(hidden_grad * prelu_slope_term(mid_norm), axis=0)
    mid_norm_grad = hidden_grad * prelu_input_factor(mid_norm, slope3)
    grad_head, grad_bias, grad_slope3, grad_gain2, grad_shift2 = lax.psum(
        (
            head_part,
            bias_part,
            slope_out_part,
            jnp.sum(mid_norm_grad * mid_hat * bucket[:, None], axis=0),
            jnp.sum(mid_norm_grad * bucket[:, None], axis=0),
        ),
        "shard",
    )
    mid_grad_low = (
        gain2
        * inv2
        * bucket[:, None]
        * (mid_norm_grad - (grad_shift2 + mid_hat * grad_gain2) / count_fill)
    ).astype(jnp.bfloat16)
    mid_part = jnp.dot(concat_low.T, mid_grad_low, preferred_element_type=jnp.float32)
    concat_grad = jnp.dot(mid_grad_low, mid_full.T, preferred_element_type=jnp.float32)
    slope_two_part = jnp.sum(concat_grad * prelu_slope_term(branch_act), axis=0)
    act_grad = concat_grad * prelu_input_factor(branch_act, slope2)
    slope_one_part = jnp.sum(act_grad * prelu_slope_term(branch_norm), axis=0)
    norm_grad = act_grad * prelu_input_factor(branch_norm, slope1)
    grad_slope1, grad_slope2, grad_gain1, grad_shift1 = lax.psum(
        (
            slope_one_part,
            slope_two_part,
            jnp.sum(norm_grad * branch_hat * bucket[:, None], axis=0),
            jnp.sum(norm_grad * bucket[:, None], axis=0),
        ),
        "shard",
    )
    branch_grad_low = (
        gain1
        * inv1
        * bucket[:, None]
        * (norm_grad - (grad_shift1 + branch_hat * grad_gain1) / count_fill)
    ).astype(jnp.bfloat16)
    branch_grad_three = branch_grad_low.reshape(node_rows, K, H)
    features_grad = jnp.einsum(
        "nkh,kfh->nkf", branch_grad_three, branch_three, preferred_element_type=jnp.float32
    ).reshape(node_rows, K * F)
    branch_part = jnp.einsum(
        "nkf,nkh->kfh", feats_three, branch_grad_three, preferred_element_type=jnp.float32
    ).reshape(K * F, H)
    grad_branch, grad_mid = (
        lax.psum_scatter(branch_part, "shard", scatter_dimension=1, tiled=True),
        lax.psum_scatter(mid_part, "shard", scatter_dimension=1, tiled=True),
    )
    grad_small = jnp.concatenate(
        [
            grad_gain1,
            grad_shift1,
            grad_slope1,
            grad_slope2,
            grad_gain2,
            grad_shift2,
            grad_slope3,
            grad_bias,
        ]
    )
    root = math.sqrt(nodes_all)
    mom_b, avg_b, new_b = nesterov(w_branch, grad_branch, mom_branch, avg_branch, 0.8 / root)
    mom_m, avg_m, new_m = nesterov(w_mid, grad_mid, mom_mid, avg_mid, 0.08 / root)
    mom_h, avg_h, new_h = nesterov(w_head, grad_head, mom_head, avg_head, 0.3 / root)
    mom_s, avg_s, new_s = nesterov(small_params, grad_small, mom_small, avg_small, 1.0 / root)
    logits = scores * bucket[:, None]
    return (
        logits,
        features_grad,
        grad_branch,
        grad_mid,
        grad_head,
        grad_small,
        mom_b,
        mom_m,
        mom_h,
        mom_s,
        avg_b,
        avg_m,
        avg_h,
        avg_s,
        new_b,
        new_m,
        new_h,
        new_s,
    )


def solution(mesh):
    in_specs = (
        P("shard", None),
        P("shard"),
        P("shard"),
        P("shard"),
        P(None, "shard"),
        P(None, "shard"),
        P(),
        P(),
        P(None, "shard"),
        P(None, "shard"),
        P(),
        P(),
        P(None, "shard"),
        P(None, "shard"),
        P(),
        P(),
    )
    out_specs = (
        P("shard", None),
        P("shard", None),
        P(None, "shard"),
        P(None, "shard"),
        P(),
        P(),
        P(None, "shard"),
        P(None, "shard"),
        P(),
        P(),
        P(None, "shard"),
        P(None, "shard"),
        P(),
        P(),
        P(None, "shard"),
        P(None, "shard"),
        P(),
        P(),
    )
    return jax.shard_map(local, mesh=mesh, in_specs=in_specs, out_specs=out_specs, check_vma=False)
```

profile of v0, /device:TPU:0, one launch (start us, length us, event | category | flops | bytes accessed | tf_op | source)
XLA Modules:
  0.0 917.9 jit_solution(16101625293680502912)
XLA Ops:
  7.2 1.5 convert_element_type.43
  11.6 44.7 %all_gather.6 = bf16[400,512]{0,1:T(8,128)(2,1)S(1)} all-gather(bf16[400,16]{0,1:T(8,128)(2,1)S(1)} %convert_element_type.40), channel_id=1, replica_groups=mesh['shard'=32] {'shard'}, dimensions={1}, use_global_device_ids=true | all-gather | bytes 422400 | tf_op jit(solution)/shard_map/all_gather | solution.py:86
  56.6 4.1 reshape.110
  60.7 18.7 %fusion.4 = (f32[4,512]{1,0:T(4,128)S(1)}, f32[4,512,5120]{2,1,0:T(8,128)}) fusion(f32[5120]{0:T(1024)S(1)} %fusion.8, bf16[4,100,512]{2,1,0:T(8,128)(2,1)S(1)} %reshape.109, bf16[5120,4,100]{0,2,1:T(8,128)(2,1)} %reshape.110), kind=kOutput, calls=%fused_computation.9 | convolution fusion | flops 2118121472 | bytes 46477312 | tf_op jit(solution)/shard_map/nkf,kfh->nkh/dot_general | solution.py:89
  79.4 37.1 %all-reduce.2 = (f32[2048]{0:T(1024)S(1)}, f32[]{:T(128)}) all-reduce(f32[2048]{0:T(1024)S(1)} %bitcast.70, f32[]{:T(128)} %fusion.9), channel_id=1, replica_groups=mesh['shard'=32] {'shard'}, use_global_device_ids=true, to_apply=%region_1.0 | all-reduce | flops 2049 | bytes 16392 | tf_op jit(solution)/shard_map/psum | solution.py:51
  117.2 16.8 %fusion.3 = f32[4,512]{1,0:T(4,128)S(1)} fusion(f32[4,512,5120]{2,1,0:T(8,128)} %get-tuple-element.129, f32[4,512]{1,0:T(4,128)S(1)} %sub.91, f32[5120]{0:T(1024)S(1)} %fusion.8), kind=kLoop, calls=%fused_computation.8 | loop fusion | flops 41940992 | bytes 41979904 | tf_op jit(solution)/shard_map/reduce_sum | solution.py:54
  134.0 42.2 %psum.103 = f32[2048]{0:T(1024)S(1)} all-reduce(f32[2048]{0:T(1024)S(1)} %bitcast.71), channel_id=1, replica_groups=mesh['shard'=32] {'shard'}, use_global_device_ids=true, to_apply=%region_5.0 | all-reduce | flops 2048 | bytes 16384 | tf_op jit(solution)/shard_map/psum | solution.py:54
  177.5 66.5 %add_convert_fusion = (bf16[5120,2048]{0,1:T(8,128)(2,1)}, f32[5120,2048]{0,1:T(8,128)}) fusion(f32[2048]{0:T(1024)S(1)} %get-tuple-element.121, f32[2048]{0:T(1024)S(1)} %get-tuple-element.127, f32[2048]{0:T(1024)S(1)} %get-tuple-element.122, f32[2048]{0:T(1024)S(1)} %get-tuple-element.125, f32[2048]{0:T(1024)S(1)} %get-tuple-element.124, ...), kind=kLoop, calls=%fused_computation.17 | loop fusion | flops 241172480 | bytes 104923136 | tf_op jit(solution)/shard_map/convert_element_type | solution.py:96
  243.9 20.0 %multiply_reduce_fusion.8 = (f32[512]{0:T(512)S(1)}, f32[5120,512]{1,0:T(8,128)}) fusion(f32[5120]{0:T(1024)S(1)} %fusion.8, bf16[5120,2048]{0,1:T(8,128)(2,1)} %get-tuple-element.108, bf16[2048,512]{0,1:T(8,128)(2,1)} %all-gather.2.cloned.1.call-done), kind=kOutput, calls=%fused_computation.29 | convolution fusion | flops 10742661120 | bytes 33576960 | tf_op jit(solution)/shard_map/dot_general | solution.py:98
  264.0 39.5 %psum.104 = f32[512]{0:T(512)S(1)} all-reduce(f32[512]{0:T(512)S(1)} %get-tuple-element.130), channel_id=1, replica_groups=mesh['shard'=32] {'shard'}, use_global_device_ids=true, to_apply=%region_7.8 | all-reduce | flops 512 | bytes 4096 | tf_op jit(solution)/shard_map/psum | solution.py:51
  304.2 5.6 multiply_reduce_fusion.7
  309.7 40.7 %psum.105 = f32[512]{0:T(512)S(1)} all-reduce(f32[512]{0:T(512)S(1)} %multiply_reduce_fusion.7), channel_id=1, replica_groups=mesh['shard'=32] {'shard'}, use_global_device_ids=true, to_apply=%region_9.10 | all-reduce | flops 512 | bytes 4096 | tf_op jit(solution)/shard_map/psum | solution.py:54
  351.1 10.0 %add_convert_fusion.1 = bf16[5120,512]{1,0:T(8,128)(2,1)S(1)} fusion(f32[5120,512]{1,0:T(8,128)} %get-tuple-element.131, f32[512]{0:T(512)S(1)} %get-tuple-element.115, f32[512]{0:T(512)S(1)} %get-tuple-element.118, f32[512]{0:T(512)S(1)} %get-tuple-element.117, f32[512]{0:T(512)S(1)} %broadcast_divide_fusion.1, f32[512]{0:T(512)S(1)} %get-tuple-element.119, ...), kind=kLoop, calls=%fused_computation.26 | loop fusion | flops 36700160 | bytes 15740928 | tf_op jit(solution)/shard_map/convert_element_type | solution.py:102
  361.1 1.6 fusion.12
  363.0 1.9 convert_reduce_fusion
  364.9 1.6 fusion.14
  366.5 16.2 %multiply_reduce_fusion.6 = (f32[512]{0:T(512)S(1)}, f32[512]{0:T(512)S(1)}, f32[512]{0:T(512)}, f32[5120,512]{1,0:T(8,128)}) fusion(f32[5120]{0:T(1024)S(1)} %fusion.8, f32[512]{0:T(512)S(1)} %get-tuple-element.118, f32[512]{0:T(512)S(1)} %get-tuple-element.117, f32[5120,512]{1,0:T(8,128)} %get-tuple-element.131, f32[512]{0:T(512)S(1)} %broadcast_divide_fusion.1, ...), kind=kOutput, calls=%fused_computation.24 | convolution fusion | flops 309352448 | bytes 21587968 | tf_op jit(solution)/shard_map/dot_general | solution.py:110
  382.8 39.8 %all-reduce.1 = (f32[512]{0:T(512)S(1)}, f32[512]{0:T(512)S(1)}) all-reduce(f32[512]{0:T(512)S(1)} %get-tuple-element.77, f32[512]{0:T(512)S(1)} %get-tuple-element.76), channel_id=1, replica_groups=mesh['shard'=32] {'shard'}, use_global_device_ids=true, to_apply=%region_15.16 | all-reduce | flops 1024 | bytes 8192 | tf_op jit(solution)/shard_map/psum | solution.py:113
  422.6 11.1 %multiply_convert_fusion.1 = bf16[5120,512]{1,0:T(8,128)(2,1)S(1)} fusion(f32[5120,512]{1,0:T(8,128)} %get-tuple-element.131, f32[]{:T(128)} %get-tuple-element.88, f32[512]{0:T(512)S(1)} %get-tuple-element.85, f32[512]{0:T(512)S(1)} %get-tuple-element.86, f32[512]{0:T(512)S(1)} %get-tuple-element.116, f32[512]{0:T(512)S(1)} %get-tuple-element.117, ...), kind=kLoop, calls=%fused_computation.22 | loop fusion | flops 44564480 | bytes 26253316 | tf_op jit(solution)/shard_map/convert_element_type | solution.py:128
  433.8 109.1 %multiply_reduce_fusion = (f32[2048]{0:T(1024)S(1)}, f32[2048]{0:T(1024)S(1)}, f32[2048]{0:T(1024)S(1)}, f32[2048]{0:T(1024)S(1)}, f32[5120,2048]{0,1:T(8,128)}) fusion(f32[5120,2048]{0,1:T(8,128)} %get-tuple-element.109, f32[2048]{0:T(1024)S(1)} %get-tuple-element.125, f32[2048]{0:T(1024)S(1)} %get-tuple-element.124, f32[2048]{0:T(1024)S(1)} %broadcast_divide_fusion, ...), kind=kOutput, calls=%fused_computation.10 | convolution fusion | flops 11146354688 | bytes 133287936 | tf_op jit(solution)/shard_map/dot_general | solution.py:130
  542.9 41.6 %all-reduce = (f32[2048]{0:T(1024)S(1)}, f32[2048]{0:T(1024)S(1)}, f32[2048]{0:T(1024)S(1)}, f32[2048]{0:T(1024)S(1)}, f32[512]{0:T(512)S(1)}, /*index=5*/f32[47]{0:T(128)S(1)}) all-reduce(f32[2048]{0:T(1024)S(1)} %get-tuple-element.110, f32[2048]{0:T(1024)S(1)} %get-tuple-element.111, ...), channel_id=1, replica_groups=mesh['shard'=32] {'shard'}, use_global_device_ids=true, to_apply=%region_19.20 | all-reduce | flops 8751 | bytes 70008 | tf_op jit(solution)/shard_map/psum | solution.py:135
  584.5 34.9 %multiply_convert_fusion = bf16[5120,2048]{0,1:T(8,128)(2,1)} fusion(f32[5120,2048]{0,1:T(8,128)} %get-tuple-element.112, f32[4,512,5120]{2,1,0:T(8,128)} %get-tuple-element.129, f32[]{:T(128)} %get-tuple-element.88, f32[2048]{0:T(1024)S(1)} %get-tuple-element.79, f32[2048]{0:T(1024)S(1)} %get-tuple-element.80, f32[5120]{0:T(1024)S(1)} %fusion.8, ...), kind=kLoop, calls=%fused_computation.12 | loop fusion | flops 94371840 | bytes 104919040 | tf_op jit(solution)/shard_map/convert_element_type | solution.py:149
  619.4 12.0 %convolution_bitcast_fusion.1 = f32[4,100,512]{2,1,0:T(8,128)S(1)} fusion(bf16[5120,4,512]{0,2,1:T(8,128)(2,1)} %bitcast.64, bf16[5120,4,100]{0,2,1:T(8,128)(2,1)} %reshape.110), kind=kOutput, calls=%fused_computation.33 | convolution fusion | flops 2097152000 | bytes 25886720 | tf_op jit(solution)/shard_map/nkf,nkh->kfh/dot_general | solution.py:154
  632.9 18.2 %fusion.13 = f32[2048,512]{0,1:T(8,128)} fusion(bf16[5120,2048]{0,1:T(8,128)(2,1)} %get-tuple-element.108, bf16[5120,512]{1,0:T(8,128)(2,1)} %copy-done), kind=kOutput, calls=%fused_computation.80 | convolution fusion | flops 10737418240 | bytes 30408704 | tf_op jit(solution)/shard_map/dot_general | solution.py:129
  651.2 12.0 %convolution_bitcast_fusion = f32[5120,4,100]{0,2,1:T(8,128)} fusion(bf16[5120,4,512]{0,2,1:T(8,128)(2,1)} %bitcast.65, bf16[4,100,512]{2,1,0:T(8,128)(2,1)S(1)} %copy-done.2), kind=kOutput, calls=%fused_computation.31 | convolution fusion | flops 2097152000 | bytes 29573120 | tf_op jit(solution)/shard_map/nkh,kfh->nkf/dot_general | solution.py:151
  663.3 9.4 %reshape.113 = f32[5120,400]{0,1:T(8,128)} reshape(f32[5120,4,100]{0,2,1:T(8,128)} %convolution_bitcast_fusion) | data formatting | bytes 16384000 | tf_op jit(solution)/shard_map/reshape | solution.py:153
  673.5 1.6 multiply_add_fusion.5
  675.1 93.1 %reduce-scatter.7.cloned.1.call-done = f32[16,400]{1,0:T(8,128)} async-done(((f32[512,400]{1,0:T(8,128)}), f32[16,400]{1,0:T(8,128)}) %reduce-scatter.7.cloned.1.call-update) | async-done | bytes 25616
  768.3 1.4 multiply_add_fusion.9
  769.7 138.3 %reduce-scatter.5.cloned.1.call-done = f32[2048,16]{0,1:T(8,128)} async-done(((f32[2048,512]{0,1:T(8,128)}), f32[2048,16]{0,1:T(8,128)}) %reduce-scatter.5.cloned.1.call-update) | async-done | bytes 131088 | tf_op jit(solution)/shard_map/reduce_scatter | solution.py:159
  908.0 1.7 multiply_add_fusion.3
  909.7 1.5 copy.83
  (92 shorter events, 8.3 us)
Async XLA Ops:
  7.2 236.7 %all-gather.2.cloned.1.call-start = ((), (), s32[]{:S(2)}) async-start(), calls=%async_computation.2 | async-start | bytes 2162688 | tf_op jit(solution)/shard_map/all_gather | solution.py:97
  8.8 664.7 %all-reduce.5.cloned.1.call-start = ((), (), s32[]{:S(2)}) async-start(), calls=%async_computation.4 | async-start | bytes 196608 | tf_op jit(solution)/shard_map/psum | solution.py:113
  56.6 22.8 %copy-start.1 = (bf16[4,100,512]{2,1,0:T(8,128)(2,1)}, bf16[4,100,512]{2,1,0:T(8,128)(2,1)S(1)}, u32[]{:S(2)}) copy-start(bf16[4,100,512]{2,1,0:T(8,128)(2,1)S(1)} %reshape.109) | copy-start | bytes 1228804
  117.1 59.0 %copy-start.6 = (f32[9775]{0:T(1024)S(1)}, f32[9775]{0:T(1024)}, u32[]{:S(2)}) copy-start(f32[9775]{0:T(1024)} %param.23) | copy-start | bytes 117304
  117.1 60.3 %copy-start.20 = (s32[5120]{0:T(1024)S(1)}, s32[5120]{0:T(1024)}, u32[]{:S(2)}) copy-start(s32[5120]{0:T(1024)} %param.18) | copy-start | bytes 61444
  309.7 51.4 %copy-start.4 = (f32[512,47]{0,1:T(8,128)S(1)}, f32[512,47]{0,1:T(8,128)}, u32[]{:S(2)}) copy-start(f32[512,47]{0,1:T(8,128)} %param.22) | copy-start | bytes 288772
  351.1 11.9 %copy-start.19 = (s32[5120]{0:T(1024)S(1)}, s32[5120]{0:T(1024)}, u32[]{:S(2)}) copy-start(s32[5120]{0:T(1024)} %param.19) | copy-start | bytes 61444
  382.7 385.5 %reduce-scatter.7.cloned.1.call-start = ((), (), s32[]{:S(2)}) async-start(), calls=%async_computation.5 | async-start | bytes 1081344
  422.6 11.1 %copy-start.21 = (f32[512]{0:T(512)}, f32[512]{0:T(512)S(1)}, u32[]{:S(2)}) copy-start(f32[512]{0:T(512)S(1)} %get-tuple-element.86) | copy-start | bytes 6148
  422.6 11.1 %copy-start.23 = (f32[512]{0:T(512)}, f32[512]{0:T(512)S(1)}, u32[]{:S(2)}) copy-start(f32[512]{0:T(512)S(1)} %get-tuple-element.85) | copy-start | bytes 6148
  433.7 109.1 %copy-start = (bf16[5120,512]{1,0:T(8,128)(2,1)}, bf16[5120,512]{1,0:T(8,128)(2,1)S(1)}, u32[]{:S(2)}) copy-start(bf16[5120,512]{1,0:T(8,128)(2,1)S(1)} %multiply_convert_fusion.1) | copy-start | bytes 15728644
  433.8 109.1 %copy-start.25 = (f32[512]{0:T(512)S(1)}, f32[512]{0:T(512)}, u32[]{:S(2)}) copy-start(f32[512]{0:T(512)} %get-tuple-element.78) | copy-start | bytes 6148
  433.8 109.1 %copy-start.26 = (f32[47]{0:T(128)S(1)}, f32[47]{0:T(128)}, u32[]{:S(2)}) copy-start(f32[47]{0:T(128)} %get-tuple-element.103) | copy-start | bytes 568
  433.8 150.7 %copy-start.16 = (f32[2048]{0:T(1024)S(1)}, f32[2048]{0:T(1024)}, u32[]{:S(2)}) copy-start(f32[2048]{0:T(1024)} %get-tuple-element.123) | copy-start | bytes 24580
  632.9 18.3 %copy-start.2 = (bf16[4,100,512]{2,1,0:T(8,128)(2,1)S(1)}, bf16[4,100,512]{2,1,0:T(8,128)(2,1)}, u32[]{:S(2)}) copy-start(bf16[4,100,512]{2,1,0:T(8,128)(2,1)} %copy-done.1) | copy-start | bytes 1228804
  632.9 275.1 %reduce-scatter.5.cloned.1.call-start = ((), (), s32[]{:S(2)}) async-start(), calls=%async_computation.3 | async-start | bytes 4325376 | tf_op jit(solution)/shard_map/reduce_scatter | solution.py:159
  663.2 9.6 %copy-start.24 = (f32[512]{0:T(512)S(1)}, f32[512]{0:T(512)}, u32[]{:S(2)}) copy-start(f32[512]{0:T(512)} %copy-done.23) | copy-start | bytes 6148
  663.2 9.6 %copy-start.22 = (f32[512]{0:T(512)S(1)}, f32[512]{0:T(512)}, u32[]{:S(2)}) copy-start(f32[512]{0:T(512)} %copy-done.21) | copy-start | bytes 6148
  663.2 9.6 %copy-start.7 = (f32[9775]{0:T(1024)S(1)}, f32[9775]{0:T(1024)}, u32[]{:S(2)}) copy-start(f32[9775]{0:T(1024)} %param.23) | copy-start | bytes 117304
  663.2 9.6 %copy-start.14 = (f32[9775]{0:T(1024)S(1)}, f32[9775]{0:T(1024)}, u32[]{:S(2)}) copy-start(f32[9775]{0:T(1024)} %param.31) | copy-start | bytes 117304
  663.2 9.6 %copy-start.15 = (f32[9775]{0:T(1024)S(1)}, f32[9775]{0:T(1024)}, u32[]{:S(2)}) copy-start(f32[9775]{0:T(1024)} %param.27) | copy-start | bytes 117304
  663.2 10.3 %copy-start.5 = (f32[512,47]{0,1:T(8,128)S(1)}, f32[512,47]{0,1:T(8,128)}, u32[]{:S(2)}) copy-start(f32[512,47]{0,1:T(8,128)} %param.22) | copy-start | bytes 288772
  663.2 10.3 %copy-start.11 = (f32[512,47]{0,1:T(8,128)S(1)}, f32[512,47]{0,1:T(8,128)}, u32[]{:S(2)}) copy-start(f32[512,47]{0,1:T(8,128)} %param.30) | copy-start | bytes 288772
  663.2 10.3 %copy-start.12 = (f32[512,47]{0,1:T(8,128)S(1)}, f32[512,47]{0,1:T(8,128)}, u32[]{:S(2)}) copy-start(f32[512,47]{0,1:T(8,128)} %param.26) | copy-start | bytes 288772
  663.2 105.1 %copy-start.10 = (f32[400,16]{0,1:T(8,128)S(1)}, f32[400,16]{0,1:T(8,128)}, u32[]{:S(2)}) copy-start(f32[400,16]{0,1:T(8,128)} %param.20) | copy-start | bytes 76804
  663.2 105.1 %copy-start.17 = (f32[400,16]{0,1:T(8,128)S(1)}, f32[400,16]{0,1:T(8,128)}, u32[]{:S(2)}) copy-start(f32[400,16]{0,1:T(8,128)} %param.28) | copy-start | bytes 76804
  663.2 105.0 %copy-start.18 = (f32[400,16]{0,1:T(8,128)S(1)}, f32[400,16]{0,1:T(8,128)}, u32[]{:S(2)}) copy-start(f32[400,16]{0,1:T(8,128)} %param.24) | copy-start | bytes 76804
  663.3 244.7 %copy-start.3 = (f32[2048,16]{0,1:T(8,128)S(1)}, f32[2048,16]{0,1:T(8,128)}, u32[]{:S(2)}) copy-start(f32[2048,16]{0,1:T(8,128)} %param.21) | copy-start | bytes 393220
  663.3 244.7 %copy-start.8 = (f32[2048,16]{0,1:T(8,128)S(1)}, f32[2048,16]{0,1:T(8,128)}, u32[]{:S(2)}) copy-start(f32[2048,16]{0,1:T(8,128)} %param.29) | copy-start | bytes 393220
  663.3 244.7 %copy-start.9 = (f32[2048,16]{0,1:T(8,128)S(1)}, f32[2048,16]{0,1:T(8,128)}, u32[]{:S(2)}) copy-start(f32[2048,16]{0,1:T(8,128)} %param.25) | copy-start | bytes 393220
  672.8 238.4 %copy-start.13 = (f32[9775]{0:T(1024)}, f32[9775]{0:T(1024)S(1)}, u32[]{:S(2)}) copy-start(f32[9775]{0:T(1024)S(1)} %constant_dynamic-update-slice_fusion) | copy-start | bytes 117304
Sparse Core Ops, SparseCore 0:
  11.5 59.4 all-gather.1
  382.9 120.6 all-reduce.4
  633.0 135.2 reduce-scatter.6
  771.1 136.8 reduce-scatter.4
where the time goes:
time: 924 us; the launch traced here: 918 us
  blocking collectives  286 us (31%)
  waiting for transfers between devices  232 us (25%)
  matrix products  209 us (23%)
  other arithmetic  158 us (17%)
  local copies, waits for them, and re-layouts  17.7 us (2%)
  between operations  15.1 us (2%)
    reduce_scatter x1, waiting for transfers between devices, local(): lax.psum_scatter(mid_part, 'shard', scatter_dimension=1, tiled=True)  138 us
    dot_general x1, matrix products, local(): jnp.dot(mid_grad_low, mid_full.T, preferred_element_type=jnp.float32)  109 us
    unnamed x5, waiting for transfers between devices  93.2 us
    psum x2, blocking collectives, moments(): lax.psum(jnp.sum(centered * centered * bucket[:, None], axis=0), 'shard')  82.9 us
    psum x2, blocking collectives, moments(): lax.psum((jnp.sum(masked, axis=0), jnp.sum(bucket)), 'shard')  76.6 us
    convert_element_type x1, other arithmetic, local(): concat_low = prelu_apply(branch_act, slope2).astype(jnp.bfloat16)  66.5 us
    all_gather x1, blocking collectives, local(): branch_full = lax.all_gather(branch_low, 'shard', axis=1, tiled=True)  44.7 us
    psum x1, blocking collectives, local(): lax.psum((slope_one_part, slope_two_part, jnp.sum(norm_grad * branch_hat...  41.6 us
  transfers between devices with their start and end apart: 4, of which 2 were waited for; matrix products, arithmetic and copies ran while one was open for 35% of the time, Pallas kernels for 0%

commit v1 on v0

--- a/solution.py
+++ b/solution.py
@@ -51,7 +51,9 @@
     totals, count_fill = lax.psum((jnp.sum(masked, axis=0), jnp.sum(bucket)), "shard")
     mean_col = totals / count_fill
     centered = columns_in - mean_col
-    squares = lax.psum(jnp.sum(centered * centered * bucket[:, None], axis=0), "shard")
+    squares = jnp.sum(
+        lax.all_gather(jnp.sum(centered * centered * bucket[:, None], axis=0), "shard"), axis=0
+    )
     variance = squares / count_fill
     return (mean_col, lax.rsqrt(variance + EPS), count_fill)
 

time: 924 us -> 918 us (level)
    psum x2 -> x0, blocking collectives: 82.9 us -> none  [moments(): lax.psum(jnp.sum(centered * centered * bucket[:, None], axis=0), 'shard')]
    all_gather x0 -> x2, blocking collectives: none -> 81.7 us  [moments(): lax.all_gather(jnp.sum(centered * centered * bucket[:, None], axis=0), 's...]
where the time goes in v1:
time: 918 us; the launch traced here: 912 us
  blocking collectives  280 us (31%)
  waiting for transfers between devices  231 us (25%)
  matrix products  209 us (23%)
  other arithmetic  159 us (17%)
  local copies, waits for them, and re-layouts  17.7 us (2%)
  between operations  15.1 us (2%)
    reduce_scatter x1, waiting for transfers between devices, local(): lax.psum_scatter(mid_part, 'shard', scatter_dimension=1, tiled=True)  138 us
    dot_general x1, matrix products, local(): jnp.dot(mid_grad_low, mid_full.T, preferred_element_type=jnp.float32)  109 us
    unnamed x5, waiting for transfers between devices  92.9 us
    all_gather x2, blocking collectives, moments(): lax.all_gather(jnp.sum(centered * centered * bucket[:, None], axis=0), 's...  81.7 us
    psum x2, blocking collectives, moments(): lax.psum((jnp.sum(masked, axis=0), jnp.sum(bucket)), 'shard')  74.1 us
    convert_element_type x1, other arithmetic, local(): concat_low = prelu_apply(branch_act, slope2).astype(jnp.bfloat16)  66.6 us
    all_gather x1, blocking collectives, local(): branch_full = lax.all_gather(branch_low, 'shard', axis=1, tiled=True)  44.7 us
    psum x1, blocking collectives, local(): lax.psum((slope_one_part, slope_two_part, jnp.sum(norm_grad * branch_hat...  41.9 us
  transfers between devices with their start and end apart: 4, of which 2 were waited for; matrix products, arithmetic and copies ran while one was open for 35% of the time, Pallas kernels for 0%

profile of v1, /device:TPU:0, one launch (start us, length us, event | category | flops | bytes accessed | tf_op | source)
XLA Modules:
  0.0 912.2 jit_solution(3993722798665691370)
XLA Ops:
  7.2 1.5 convert_element_type.43
  11.6 44.7 %all_gather.18 = bf16[400,512]{0,1:T(8,128)(2,1)S(1)} all-gather(bf16[400,16]{0,1:T(8,128)(2,1)S(1)} %convert_element_type.40), channel_id=1, replica_groups=mesh['shard'=32] {'shard'}, dimensions={1}, use_global_device_ids=true | all-gather | bytes 422400 | tf_op jit(solution)/shard_map/all_gather | solution.py:88
  56.6 4.1 reshape.119
  60.7 18.7 %fusion.4 = (f32[4,512]{1,0:T(4,128)S(1)}, f32[4,512,5120]{2,1,0:T(8,128)}) fusion(f32[5120]{0:T(1024)S(1)} %fusion.8, bf16[4,100,512]{2,1,0:T(8,128)(2,1)S(1)} %reshape.118, bf16[5120,4,100]{0,2,1:T(8,128)(2,1)} %reshape.119), kind=kOutput, calls=%fused_computation.9 | convolution fusion | flops 2118121472 | bytes 46477312 | tf_op jit(solution)/shard_map/nkf,kfh->nkh/dot_general | solution.py:91
  79.4 37.1 %all-reduce.2 = (f32[2048]{0:T(1024)S(1)}, f32[]{:T(128)}) all-reduce(f32[2048]{0:T(1024)S(1)} %bitcast.68, f32[]{:T(128)} %fusion.9), channel_id=1, replica_groups=mesh['shard'=32] {'shard'}, use_global_device_ids=true, to_apply=%region_1.0 | all-reduce | flops 2049 | bytes 16392 | tf_op jit(solution)/shard_map/psum | solution.py:51
  117.2 16.8 %fusion.3 = f32[4,512]{1,0:T(4,128)S(1)} fusion(f32[4,512,5120]{2,1,0:T(8,128)} %get-tuple-element.129, f32[4,512]{1,0:T(4,128)S(1)} %sub.91, f32[5120]{0:T(1024)S(1)} %fusion.8), kind=kLoop, calls=%fused_computation.8 | loop fusion | flops 41940992 | bytes 41979904 | tf_op jit(solution)/shard_map/reduce_sum | solution.py:55
  134.0 41.2 %all-gather.1 = f32[32,1,2048]{2,1,0:T(1,128)S(1)} all-gather(f32[1,1,2048]{2,1,0:T(1,128)S(1)} %reshape.125), channel_id=1, replica_groups=mesh['shard'=32] {'shard'}, dimensions={0}, use_global_device_ids=true | all-gather | bytes 270336 | tf_op jit(solution)/shard_map/all_gather | solution.py:55
  176.7 66.6 %add_convert_fusion = (bf16[5120,2048]{0,1:T(8,128)(2,1)}, f32[5120,2048]{0,1:T(8,128)}) fusion(f32[2048]{0:T(1024)S(1)} %get-tuple-element.121, f32[2048]{0:T(1024)S(1)} %get-tuple-element.127, f32[2048]{0:T(1024)S(1)} %get-tuple-element.122, f32[2048]{0:T(1024)S(1)} %get-tuple-element.125, f32[2048]{0:T(1024)S(1)} %get-tuple-element.124, ...), kind=kLoop, calls=%fused_computation.17 | loop fusion | flops 241172480 | bytes 104923136 | tf_op jit(solution)/shard_map/convert_element_type | solution.py:98
  243.3 19.9 %multiply_reduce_fusion.8 = (f32[512]{0:T(512)S(1)}, f32[5120,512]{1,0:T(8,128)}) fusion(f32[5120]{0:T(1024)S(1)} %fusion.8, bf16[5120,2048]{0,1:T(8,128)(2,1)} %get-tuple-element.108, bf16[2048,512]{0,1:T(8,128)(2,1)} %all-gather.5.cloned.1.call-done), kind=kOutput, calls=%fused_computation.29 | convolution fusion | flops 10742661120 | bytes 33576960 | tf_op jit(solution)/shard_map/dot_general | solution.py:100
  263.2 37.0 %psum.89 = f32[512]{0:T(512)S(1)} all-reduce(f32[512]{0:T(512)S(1)} %get-tuple-element.130), channel_id=1, replica_groups=mesh['shard'=32] {'shard'}, use_global_device_ids=true, to_apply=%region_7.8 | all-reduce | flops 512 | bytes 4096 | tf_op jit(solution)/shard_map/psum | solution.py:51
  300.9 5.6 multiply_reduce_fusion.7
  306.4 40.5 %all-gather.2 = f32[32,1,512]{2,1,0:T(1,128)S(1)} all-gather(f32[1,1,512]{2,1,0:T(1,128)S(1)} %bitcast.69), channel_id=2, replica_groups=mesh['shard'=32] {'shard'}, dimensions={0}, use_global_device_ids=true | all-gather | bytes 67584 | tf_op jit(solution)/shard_map/all_gather | solution.py:55
  347.7 10.0 %add_convert_fusion.1 = bf16[5120,512]{1,0:T(8,128)(2,1)S(1)} fusion(f32[5120,512]{1,0:T(8,128)} %get-tuple-element.131, f32[512]{0:T(512)S(1)} %get-tuple-element.115, f32[512]{0:T(512)S(1)} %get-tuple-element.118, f32[512]{0:T(512)S(1)} %get-tuple-element.117, f32[512]{0:T(512)S(1)} %broadcast_divide_fusion.1, f32[512]{0:T(512)S(1)} %get-tuple-element.119, ...), kind=kLoop, calls=%fused_computation.26 | loop fusion | flops 36700160 | bytes 15740928 | tf_op jit(solution)/shard_map/convert_element_type | solution.py:104
  357.7 1.6 fusion.12
  359.6 1.9 convert_reduce_fusion
  361.5 1.6 fusion.14
  363.1 16.2 %multiply_reduce_fusion.6 = (f32[512]{0:T(512)S(1)}, f32[512]{0:T(512)S(1)}, f32[512]{0:T(512)}, f32[5120,512]{1,0:T(8,128)}) fusion(f32[5120]{0:T(1024)S(1)} %fusion.8, f32[512]{0:T(512)S(1)} %get-tuple-element.118, f32[512]{0:T(512)S(1)} %get-tuple-element.117, f32[5120,512]{1,0:T(8,128)} %get-tuple-element.131, f32[512]{0:T(512)S(1)} %broadcast_divide_fusion.1, ...), kind=kOutput, calls=%fused_computation.24 | convolution fusion | flops 309352448 | bytes 21587968 | tf_op jit(solution)/shard_map/dot_general | solution.py:112
  379.4 37.4 %all-reduce.1 = (f32[512]{0:T(512)S(1)}, f32[512]{0:T(512)S(1)}) all-reduce(f32[512]{0:T(512)S(1)} %get-tuple-element.77, f32[512]{0:T(512)S(1)} %get-tuple-element.76), channel_id=1, replica_groups=mesh['shard'=32] {'shard'}, use_global_device_ids=true, to_apply=%region_15.16 | all-reduce | flops 1024 | bytes 8192 | tf_op jit(solution)/shard_map/psum | solution.py:115
  416.8 11.1 %multiply_convert_fusion.1 = bf16[5120,512]{1,0:T(8,128)(2,1)S(1)} fusion(f32[5120,512]{1,0:T(8,128)} %get-tuple-element.131, f32[]{:T(128)} %get-tuple-element.88, f32[512]{0:T(512)S(1)} %get-tuple-element.85, f32[512]{0:T(512)S(1)} %get-tuple-element.86, f32[512]{0:T(512)S(1)} %get-tuple-element.116, f32[512]{0:T(512)S(1)} %get-tuple-element.117, ...), kind=kLoop, calls=%fused_computation.22 | loop fusion | flops 44564480 | bytes 26253316 | tf_op jit(solution)/shard_map/convert_element_type | solution.py:130
  428.0 109.1 %multiply_reduce_fusion = (f32[2048]{0:T(1024)S(1)}, f32[2048]{0:T(1024)S(1)}, f32[2048]{0:T(1024)S(1)}, f32[2048]{0:T(1024)S(1)}, f32[5120,2048]{0,1:T(8,128)}) fusion(f32[5120,2048]{0,1:T(8,128)} %get-tuple-element.109, f32[2048]{0:T(1024)S(1)} %get-tuple-element.125, f32[2048]{0:T(1024)S(1)} %get-tuple-element.124, f32[2048]{0:T(1024)S(1)} %broadcast_divide_fusion, ...), kind=kOutput, calls=%fused_computation.10 | convolution fusion | flops 11146354688 | bytes 133287936 | tf_op jit(solution)/shard_map/dot_general | solution.py:132
  537.1 41.9 %all-reduce = (f32[2048]{0:T(1024)S(1)}, f32[2048]{0:T(1024)S(1)}, f32[2048]{0:T(1024)S(1)}, f32[2048]{0:T(1024)S(1)}, f32[512]{0:T(512)S(1)}, /*index=5*/f32[47]{0:T(128)S(1)}) all-reduce(f32[2048]{0:T(1024)S(1)} %get-tuple-element.110, f32[2048]{0:T(1024)S(1)} %get-tuple-element.111, ...), channel_id=1, replica_groups=mesh['shard'=32] {'shard'}, use_global_device_ids=true, to_apply=%region_19.20 | all-reduce | flops 8751 | bytes 70008 | tf_op jit(solution)/shard_map/psum | solution.py:137
  578.9 34.9 %multiply_convert_fusion = bf16[5120,2048]{0,1:T(8,128)(2,1)} fusion(f32[5120,2048]{0,1:T(8,128)} %get-tuple-element.112, f32[4,512,5120]{2,1,0:T(8,128)} %get-tuple-element.129, f32[]{:T(128)} %get-tuple-element.88, f32[2048]{0:T(1024)S(1)} %get-tuple-element.79, f32[2048]{0:T(1024)S(1)} %get-tuple-element.80, f32[5120]{0:T(1024)S(1)} %fusion.8, ...), kind=kLoop, calls=%fused_computation.12 | loop fusion | flops 94371840 | bytes 104919040 | tf_op jit(solution)/shard_map/convert_element_type | solution.py:151
  613.9 12.0 %convolution_bitcast_fusion.1 = f32[4,100,512]{2,1,0:T(8,128)S(1)} fusion(bf16[5120,4,512]{0,2,1:T(8,128)(2,1)} %bitcast.63, bf16[5120,4,100]{0,2,1:T(8,128)(2,1)} %reshape.119), kind=kOutput, calls=%fused_computation.33 | convolution fusion | flops 2097152000 | bytes 25886720 | tf_op jit(solution)/shard_map/nkf,nkh->kfh/dot_general | solution.py:156
  627.4 18.2 %fusion.13 = f32[2048,512]{0,1:T(8,128)} fusion(bf16[5120,2048]{0,1:T(8,128)(2,1)} %get-tuple-element.108, bf16[5120,512]{1,0:T(8,128)(2,1)} %copy-done), kind=kOutput, calls=%fused_computation.80 | convolution fusion | flops 10737418240 | bytes 30408704 | tf_op jit(solution)/shard_map/dot_general | solution.py:131
  645.7 12.0 %convolution_bitcast_fusion = f32[5120,4,100]{0,2,1:T(8,128)} fusion(bf16[5120,4,512]{0,2,1:T(8,128)(2,1)} %bitcast.64, bf16[4,100,512]{2,1,0:T(8,128)(2,1)S(1)} %copy-done.2), kind=kOutput, calls=%fused_computation.31 | convolution fusion | flops 2097152000 | bytes 29573120 | tf_op jit(solution)/shard_map/nkh,kfh->nkf/dot_general | solution.py:153
  657.8 9.4 %reshape.122 = f32[5120,400]{0,1:T(8,128)} reshape(f32[5120,4,100]{0,2,1:T(8,128)} %convolution_bitcast_fusion) | data formatting | bytes 16384000 | tf_op jit(solution)/shard_map/reshape | solution.py:155
  668.0 1.6 multiply_add_fusion.5
  669.6 92.8 %reduce-scatter.7.cloned.1.call-done = f32[16,400]{1,0:T(8,128)} async-done(((f32[512,400]{1,0:T(8,128)}), f32[16,400]{1,0:T(8,128)}) %reduce-scatter.7.cloned.1.call-update) | async-done | bytes 25616
  762.5 1.4 multiply_add_fusion.9
  763.9 138.3 %reduce-scatter.5.cloned.1.call-done = f32[2048,16]{0,1:T(8,128)} async-done(((f32[2048,512]{0,1:T(8,128)}), f32[2048,16]{0,1:T(8,128)}) %reduce-scatter.5.cloned.1.call-update) | async-done | bytes 131088 | tf_op jit(solution)/shard_map/reduce_scatter | solution.py:161
  902.2 1.7 multiply_add_fusion.3
  903.9 1.5 copy.82
  (94 shorter events, 8.5 us)
Async XLA Ops:
  7.2 236.1 %all-gather.5.cloned.1.call-start = ((), (), s32[]{:S(2)}) async-start(), calls=%async_computation.2 | async-start | bytes 2162688 | tf_op jit(solution)/shard_map/all_gather | solution.py:99
  8.8 659.2 %all-reduce.5.cloned.1.call-start = ((), (), s32[]{:S(2)}) async-start(), calls=%async_computation.4 | async-start | bytes 196608 | tf_op jit(solution)/shard_map/psum | solution.py:115
  56.6 22.8 %copy-start.1 = (bf16[4,100,512]{2,1,0:T(8,128)(2,1)}, bf16[4,100,512]{2,1,0:T(8,128)(2,1)S(1)}, u32[]{:S(2)}) copy-start(bf16[4,100,512]{2,1,0:T(8,128)(2,1)S(1)} %reshape.118) | copy-start | bytes 1228804
  117.1 58.3 %copy-start.6 = (f32[9775]{0:T(1024)S(1)}, f32[9775]{0:T(1024)}, u32[]{:S(2)}) copy-start(f32[9775]{0:T(1024)} %param.23) | copy-start | bytes 117304
  117.1 59.5 %copy-start.20 = (s32[5120]{0:T(1024)S(1)}, s32[5120]{0:T(1024)}, u32[]{:S(2)}) copy-start(s32[5120]{0:T(1024)} %param.18) | copy-start | bytes 61444
  306.4 51.3 %copy-start.4 = (f32[512,47]{0,1:T(8,128)S(1)}, f32[512,47]{0,1:T(8,128)}, u32[]{:S(2)}) copy-start(f32[512,47]{0,1:T(8,128)} %param.22) | copy-start | bytes 288772
  347.7 11.9 %copy-start.19 = (s32[5120]{0:T(1024)S(1)}, s32[5120]{0:T(1024)}, u32[]{:S(2)}) copy-start(s32[5120]{0:T(1024)} %param.19) | copy-start | bytes 61444
  379.3 383.2 %reduce-scatter.7.cloned.1.call-start = ((), (), s32[]{:S(2)}) async-start(), calls=%async_computation.5 | async-start | bytes 1081344
  416.8 11.1 %copy-start.21 = (f32[512]{0:T(512)}, f32[512]{0:T(512)S(1)}, u32[]{:S(2)}) copy-start(f32[512]{0:T(512)S(1)} %get-tuple-element.86) | copy-start | bytes 6148
  416.8 11.1 %copy-start.23 = (f32[512]{0:T(512)}, f32[512]{0:T(512)S(1)}, u32[]{:S(2)}) copy-start(f32[512]{0:T(512)S(1)} %get-tuple-element.85) | copy-start | bytes 6148
  427.9 109.1 %copy-start = (bf16[5120,512]{1,0:T(8,128)(2,1)}, bf16[5120,512]{1,0:T(8,128)(2,1)S(1)}, u32[]{:S(2)}) copy-start(bf16[5120,512]{1,0:T(8,128)(2,1)S(1)} %multiply_convert_fusion.1) | copy-start | bytes 15728644
  427.9 109.1 %copy-start.25 = (f32[512]{0:T(512)S(1)}, f32[512]{0:T(512)}, u32[]{:S(2)}) copy-start(f32[512]{0:T(512)} %get-tuple-element.78) | copy-start | bytes 6148
  427.9 109.1 %copy-start.26 = (f32[47]{0:T(128)S(1)}, f32[47]{0:T(128)}, u32[]{:S(2)}) copy-start(f32[47]{0:T(128)} %get-tuple-element.103) | copy-start | bytes 568
  428.0 151.0 %copy-start.16 = (f32[2048]{0:T(1024)S(1)}, f32[2048]{0:T(1024)}, u32[]{:S(2)}) copy-start(f32[2048]{0:T(1024)} %get-tuple-element.123) | copy-start | bytes 24580
  627.3 18.3 %copy-start.2 = (bf16[4,100,512]{2,1,0:T(8,128)(2,1)S(1)}, bf16[4,100,512]{2,1,0:T(8,128)(2,1)}, u32[]{:S(2)}) copy-start(bf16[4,100,512]{2,1,0:T(8,128)(2,1)} %copy-done.1) | copy-start | bytes 1228804
  627.4 274.8 %reduce-scatter.5.cloned.1.call-start = ((), (), s32[]{:S(2)}) async-start(), calls=%async_computation.3 | async-start | bytes 4325376 | tf_op jit(solution)/shard_map/reduce_scatter | solution.py:161
  657.7 9.6 %copy-start.24 = (f32[512]{0:T(512)S(1)}, f32[512]{0:T(512)}, u32[]{:S(2)}) copy-start(f32[512]{0:T(512)} %copy-done.23) | copy-start | bytes 6148
  657.7 9.6 %copy-start.22 = (f32[512]{0:T(512)S(1)}, f32[512]{0:T(512)}, u32[]{:S(2)}) copy-start(f32[512]{0:T(512)} %copy-done.21) | copy-start | bytes 6148
  657.7 9.6 %copy-start.7 = (f32[9775]{0:T(1024)S(1)}, f32[9775]{0:T(1024)}, u32[]{:S(2)}) copy-start(f32[9775]{0:T(1024)} %param.23) | copy-start | bytes 117304
  657.7 9.6 %copy-start.14 = (f32[9775]{0:T(1024)S(1)}, f32[9775]{0:T(1024)}, u32[]{:S(2)}) copy-start(f32[9775]{0:T(1024)} %param.31) | copy-start | bytes 117304
  657.7 9.6 %copy-start.15 = (f32[9775]{0:T(1024)S(1)}, f32[9775]{0:T(1024)}, u32[]{:S(2)}) copy-start(f32[9775]{0:T(1024)} %param.27) | copy-start | bytes 117304
  657.7 10.3 %copy-start.5 = (f32[512,47]{0,1:T(8,128)S(1)}, f32[512,47]{0,1:T(8,128)}, u32[]{:S(2)}) copy-start(f32[512,47]{0,1:T(8,128)} %param.22) | copy-start | bytes 288772
  657.7 10.3 %copy-start.11 = (f32[512,47]{0,1:T(8,128)S(1)}, f32[512,47]{0,1:T(8,128)}, u32[]{:S(2)}) copy-start(f32[512,47]{0,1:T(8,128)} %param.30) | copy-start | bytes 288772
  657.7 10.3 %copy-start.12 = (f32[512,47]{0,1:T(8,128)S(1)}, f32[512,47]{0,1:T(8,128)}, u32[]{:S(2)}) copy-start(f32[512,47]{0,1:T(8,128)} %param.26) | copy-start | bytes 288772
  657.7 104.7 %copy-start.10 = (f32[400,16]{0,1:T(8,128)S(1)}, f32[400,16]{0,1:T(8,128)}, u32[]{:S(2)}) copy-start(f32[400,16]{0,1:T(8,128)} %param.20) | copy-start | bytes 76804
  657.7 104.7 %copy-start.17 = (f32[400,16]{0,1:T(8,128)S(1)}, f32[400,16]{0,1:T(8,128)}, u32[]{:S(2)}) copy-start(f32[400,16]{0,1:T(8,128)} %param.28) | copy-start | bytes 76804
  657.8 104.7 %copy-start.18 = (f32[400,16]{0,1:T(8,128)S(1)}, f32[400,16]{0,1:T(8,128)}, u32[]{:S(2)}) copy-start(f32[400,16]{0,1:T(8,128)} %param.24) | copy-start | bytes 76804
  657.8 244.4 %copy-start.3 = (f32[2048,16]{0,1:T(8,128)S(1)}, f32[2048,16]{0,1:T(8,128)}, u32[]{:S(2)}) copy-start(f32[2048,16]{0,1:T(8,128)} %param.21) | copy-start | bytes 393220
  657.8 244.4 %copy-start.8 = (f32[2048,16]{0,1:T(8,128)S(1)}, f32[2048,16]{0,1:T(8,128)}, u32[]{:S(2)}) copy-start(f32[2048,16]{0,1:T(8,128)} %param.29) | copy-start | bytes 393220
  657.8 244.4 %copy-start.9 = (f32[2048,16]{0,1:T(8,128)S(1)}, f32[2048,16]{0,1:T(8,128)}, u32[]{:S(2)}) copy-start(f32[2048,16]{0,1:T(8,128)} %param.25) | copy-start | bytes 393220
  667.3 238.1 %copy-start.13 = (f32[9775]{0:T(1024)}, f32[9775]{0:T(1024)S(1)}, u32[]{:S(2)}) copy-start(f32[9775]{0:T(1024)S(1)} %constant_dynamic-update-slice_fusion) | copy-start | bytes 117304
Sparse Core Ops, SparseCore 0:
  11.5 59.4 all-gather.4
  379.4 116.7 all-reduce.4
  627.5 134.9 reduce-scatter.6
  765.3 136.8 reduce-scatter.4
